TPU v7x, 256 devices: a whole 4x4x8 slice. The times are simulated.
256 devices in a mesh: rep: 4 (over y_hi, core), fsdp: 64 (over z, y_lo, x).
Axes of the slice: x: 4, y: 4 (y_hi: 2, y_lo: 2; y = y_hi * 2 + y_lo), z: 8, core: 2. Of those that a mesh axis runs over, the one named last changes fastest.
Arguments:
- tokens_in: bfloat16 [4096, 4096], P(('rep', 'fsdp')), may hold values from -6 to 6
- cotangent: bfloat16 [4096, 4096], P(('rep', 'fsdp')), may hold values from -12 to 12
- gate_weight: bfloat16 [4, 7168, 4096], P('rep', 'fsdp'), may hold values from -6 to 6
- up_master: float32 [4, 7168, 4096], P('rep', 'fsdp'), may hold values from -6 to 6
- down_weight: bfloat16 [4, 7168, 4096], P('rep', 'fsdp'), may hold values from -6 to 6
- up_first: bfloat16 [4, 7168, 4096], P('rep', 'fsdp'), may hold values from -4 to 4
- up_second: bfloat16 [4, 7168, 4096], P('rep', 'fsdp'), may hold values from 0.019897461 to 1
- snapshot: bfloat16 [4, 4096, 4096], P('rep', 'fsdp'), may hold values from -6 to 6
- global_params: float32 [4096, 4096], P('fsdp', 'rep'), may hold values from -6 to 6
- outer_momentum: float32 [4096, 4096], P('fsdp', 'rep'), may hold values from -4 to 4
Outputs:
- input_grad: bfloat16 [4096, 4096], P(('rep', 'fsdp'))
- up_new: float32 [4, 7168, 4096], P('rep', 'fsdp')
- first_new: bfloat16 [4, 7168, 4096], P('rep', 'fsdp')
- second_new: bfloat16 [4, 7168, 4096], P('rep', 'fsdp')
- global_new: float32 [4096, 4096], P('fsdp', 'rep')
- momentum_new: float32 [4096, 4096], P('fsdp', 'rep')
All inputs are finite; a program needn't handle non-finite values.
Results may differ from a plain program's by a relative error of at most 0.009.
Values may be sent and summed in bfloat16 or wider, within the bound.
No kernel may reach another device: no remote copies, remote signals or barrier semaphores. Data moves between devices by JAX's collectives and lax.ppermute only.
A program may use at most 128 MiB of HBM per device.

v0:
```python
import math
import jax
import jax.numpy as jnp
from jax import lax
from jax.sharding import PartitionSpec as P

D = 4096
FFW = 7168
beta_one = 0.9
beta_two = 0.95
inner_rate = 0.02
decay_rate = 0.1
adam_eps = 1e-08
bias_one = 0.9999734386011124
bias_two = 0.9940794707796659
outer_rate = 0.7
outer_mu = 0.9


def by_rows(left, right):
    return lax.dot_general(
        left, right, (((1,), (1,)), ((), ())), preferred_element_type=jnp.float32
    )


def local(
    tokens_in,
    cotangent,
    gate_weight,
    up_master,
    down_weight,
    up_first,
    up_second,
    snapshot,
    global_params,
    outer_momentum,
):
    in_scale = 1.0 / math.sqrt(D)
    hid_scale = 1.0 / math.sqrt(FFW)
    w_gate = gate_weight[0]
    w_master = up_master[0]
    w_down = down_weight[0]
    w_up = w_master.astype(jnp.bfloat16)
    gathered, out_grads = (
        lax.all_gather(tokens_in, "fsdp", axis=0, tiled=True),
        lax.all_gather(cotangent, "fsdp", axis=0, tiled=True),
    )
    hid_grad = by_rows(out_grads, w_down) * hid_scale
    pre_gate = by_rows(gathered, w_gate) * in_scale
    pre_up = by_rows(gathered, w_up) * in_scale
    sigma = jax.nn.sigmoid(pre_gate)
    up_grad = (hid_grad * pre_gate * sigma).astype(jnp.bfloat16)
    gate_grad = (hid_grad * pre_up * sigma * (1.0 + pre_gate * (1.0 - sigma))).astype(jnp.bfloat16)
    weight_grad = (
        lax.dot_general(
            up_grad, gathered, (((0,), (0,)), ((), ())), preferred_element_type=jnp.float32
        )
        * in_scale
    )
    input_grad = lax.psum_scatter(
        (
            jnp.dot(gate_grad, w_gate, preferred_element_type=jnp.float32)
            + jnp.dot(up_grad, w_up, preferred_element_type=jnp.float32)
        )
        * in_scale,
        "fsdp",
        scatter_dimension=0,
        tiled=True,
    ).astype(jnp.bfloat16)
    first = beta_one * up_first[0].astype(jnp.float32) + (1.0 - beta_one) * weight_grad
    second = (
        beta_two * up_second[0].astype(jnp.float32) + (1.0 - beta_two) * weight_grad * weight_grad
    )
    updated = w_master * (1.0 - inner_rate * decay_rate) - inner_rate * (first / bias_one) / (
        jnp.sqrt(second / bias_two) + adam_eps
    )
    own_snap = snapshot[0].astype(jnp.float32)
    summed = lax.psum(own_snap.astype(jnp.bfloat16), "rep").astype(jnp.float32)
    columns = global_params.shape[1]
    summed = lax.dynamic_slice_in_dim(summed, lax.axis_index("rep") * columns, columns, 1)
    delta = global_params - summed / lax.axis_size("rep")
    momentum_new = outer_mu * outer_momentum + delta
    global_new = global_params - outer_rate * (delta + outer_mu * momentum_new)
    return (
        input_grad,
        updated[None],
        first.astype(jnp.bfloat16)[None],
        second.astype(jnp.bfloat16)[None],
        global_new,
        momentum_new,
    )


def solution(mesh):
    in_specs = (
        P(("rep", "fsdp"), None),
        P(("rep", "fsdp"), None),
        P("rep", "fsdp", None),
        P("rep", "fsdp", None),
        P("rep", "fsdp", None),
        P("rep", "fsdp", None),
        P("rep", "fsdp", None),
        P("rep", "fsdp", None),
        P("fsdp", "rep"),
        P("fsdp", "rep"),
    )
    out_specs = (
        P(("rep", "fsdp"), None),
        P("rep", "fsdp", None),
        P("rep", "fsdp", None),
        P("rep", "fsdp", None),
        P("fsdp", "rep"),
        P("fsdp", "rep"),
    )
    return jax.shard_map(local, mesh=mesh, in_specs=in_specs, out_specs=out_specs, check_vma=False)
```

profile of v0, /device:TPU:16, one launch (start us, length us, event | category | flops | bytes accessed | tf_op | source)
XLA Modules:
  0.0 1034.1 jit_solution(8883884559133859501)
XLA Ops:
  8.0 0.0 copy-start
  8.0 0.0 all-gather.5.cloned.1.call-start
  8.1 0.7 all-gather.5.cloned.1.call-update
  8.7 0.0 all-gather.3.cloned.1.call-start
  8.8 0.7 all-gather.3.cloned.1.call-update
  9.5 0.0 all-reduce.2.cloned.1.call-start
  9.5 0.5 all-reduce.2.cloned.1.call-update
  10.1 0.0 reduce-scatter.2.cloned.1.call-start
  10.1 314.8 %all-gather.5.cloned.1.call-done = bf16[1024,4096]{1,0:T(8,128)(2,1)} async-done(((bf16[16,4096]{1,0:T(8,128)(2,1)}), bf16[1024,4096]{1,0:T(8,128)(2,1)}) %all-gather.5.cloned.1.call-update) | async-done | bytes 8388624 | tf_op jit(solution)/shard_map/all_gather | solution.py:45
  325.0 0.0 copy-done
  325.0 6.2 convolution_multiply_fusion
  331.2 0.0 copy-start.1
  331.2 305.1 %all-gather.3.cloned.1.call-done = bf16[1024,4096]{1,0:T(8,128)(2,1)} async-done(((bf16[16,4096]{1,0:T(8,128)(2,1)}), bf16[1024,4096]{1,0:T(8,128)(2,1)}) %all-gather.3.cloned.1.call-update) | async-done | bytes 8388624 | tf_op jit(solution)/shard_map/all_gather | solution.py:46
  636.2 7.2 multiply_convert_fusion
  643.4 0.0 copy-done.1
  643.4 14.6 %fusion.5 = f32[1024,4096]{1,0:T(8,128)} fusion(f32[1024,112]{0,1:T(8,128)} %get-tuple-element.12, bf16[1024,4096]{1,0:T(8,128)(2,1)} %all-gather.5.cloned.1.call-done, bf16[1,112,4096]{2,1,0:T(8,128)(2,1)S(1)} %copy-done, f32[1024,112]{0,1:T(8,128)S(1)} %convolution_multiply_fusion, f32[1,112,4096]{2,1,0:T(8,128)S(1)} %copy-done.1), kind=kOutput, calls=%fused_computation.12 | convolution fusion | flops 1880768512 | bytes 28835840 | tf_op jit(solution)/shard_map/dot_general | solution.py:62
  658.0 13.9 %add_multiply_fusion = f32[1024,4096]{1,0:T(8,128)} fusion(f32[1024,4096]{1,0:T(8,128)} %fusion.5, bf16[1024,112]{0,1:T(8,128)(2,1)S(1)} %get-tuple-element.11, f32[1,112,4096]{2,1,0:T(8,128)S(1)} %copy-done.1), kind=kOutput, calls=%fused_computation | convolution fusion | flops 948371456 | bytes 35618816 | tf_op jit(solution)/shard_map/dot_general | solution.py:63
  671.9 0.0 copy-start.2
  671.9 0.0 copy-start.3
  671.9 0.0 reduce-scatter.2.cloned.1.call-update
  672.0 0.0 all-reduce.2.cloned.1.call-done
  672.0 0.9 copy-done.2
  672.9 0.1 copy-done.3
  672.9 1.8 multiply_subtract_fusion
  674.7 8.6 convert_bitcast_fusion
  683.4 341.9 %reduce-scatter.2.cloned.1.call-done = f32[16,4096]{1,0:T(8,128)} async-done(((f32[1024,4096]{1,0:T(8,128)}), f32[16,4096]{1,0:T(8,128)}) %reduce-scatter.2.cloned.1.call-update) | async-done | bytes 262160 | tf_op jit(solution)/shard_map/reduce_scatter | solution.py:60
  1025.3 1.6 convert_element_type.38
Async XLA Ops:
  8.0 317.0 %copy-start = (bf16[1,112,4096]{2,1,0:T(8,128)(2,1)S(1)}, bf16[1,112,4096]{2,1,0:T(8,128)(2,1)}, u32[]{:S(2)}) copy-start(bf16[1,112,4096]{2,1,0:T(8,128)(2,1)} %param.12) | copy-start | bytes 2752516
  8.0 317.0 %all-gather.5.cloned.1.call-start = ((), (), s32[]{:S(2)}) async-start(), calls=%async_computation.2 | async-start | bytes 8519680 | tf_op jit(solution)/shard_map/all_gather | solution.py:45
  8.7 627.5 %all-gather.3.cloned.1.call-start = ((), (), s32[]{:S(2)}) async-start(), calls=%async_computation.1 | async-start | bytes 8519680 | tf_op jit(solution)/shard_map/all_gather | solution.py:46
  9.5 662.5 %all-reduce.2.cloned.1.call-start = ((), (), s32[]{:S(2)}) async-start(), calls=%async_computation.4 | async-start | bytes 1048576 | tf_op jit(solution)/shard_map/psum | solution.py:78
  10.1 1015.2 %reduce-scatter.2.cloned.1.call-start = ((), (), s32[]{:S(2)}) async-start(), calls=%async_computation.3 | async-start | bytes 17039360 | tf_op jit(solution)/shard_map/reduce_scatter | solution.py:60
  331.2 312.3 %copy-start.1 = (f32[1,112,4096]{2,1,0:T(8,128)S(1)}, f32[1,112,4096]{2,1,0:T(8,128)}, u32[]{:S(2)}) copy-start(f32[1,112,4096]{2,1,0:T(8,128)} %param.13) | copy-start | bytes 5505028
  671.9 0.9 copy-start.2
  671.9 1.0 copy-start.3
Sparse Core Ops, SparseCore 0:
  10.6 314.2 all-gather.4
  326.8 309.4 all-gather.2
  672.1 353.1 reduce-scatter.1
Sparse Core Ops, SparseCore 1:
  12.6 50.6 all-reduce.1
where the time goes:
time: 1030 us
  waiting for transfers between devices  964 us (94%)
  matrix products  50.5 us (5%)
  between operations  15.2 us (1%)
    reduce_scatter x1, waiting for transfers between devices, local(): lax.psum_scatter((jnp.dot(gate_grad, w_gate, preferred_element_type=jnp.f...  342 us
    all_gather x1, waiting for transfers between devices, local(): lax.all_gather(tokens_in, 'fsdp', axis=0, tiled=True)  315 us
    all_gather x1, waiting for transfers between devices, local(): lax.all_gather(cotangent, 'fsdp', axis=0, tiled=True)  305 us
  transfers between devices with their start and end apart: 4, of which 3 were waited for; matrix products, arithmetic and copies ran while one was open for 5% of the time, Pallas kernels for 0%

commit v1 on v0

--- a/solution.py
+++ b/solution.py
@@ -43,7 +43,9 @@
     w_up = w_master.astype(jnp.bfloat16)
     gathered, out_grads = (
         lax.all_gather(tokens_in, "fsdp", axis=0, tiled=True),
-        lax.all_gather(cotangent, "fsdp", axis=0, tiled=True),
+        jnp.concatenate(
+            lax.all_to_all(jnp.stack([cotangent] * lax.axis_size("fsdp")), "fsdp", 0, 0), axis=0
+        ),
     )
     hid_grad = by_rows(out_grads, w_down) * hid_scale
     pre_gate = by_rows(gathered, w_gate) * in_scale

time: 1030 us -> 806 us (0.78)
  waiting for transfers between devices: 964 us -> 717 us
  starting transfers between devices: 0.16 us -> 13 us
    all_gather x1 -> x0, waiting for transfers between devices: 305 us -> none  [local(): lax.all_gather(cotangent, 'fsdp', axis=0, tiled=True)]
    all_gather x1, waiting for transfers between devices: 315 us -> 368 us  [local(): lax.all_gather(tokens_in, 'fsdp', axis=0, tiled=True)]
    all_to_all x0 -> x1, starting transfers between devices: none -> 12.9 us  [local(): lax.all_to_all(jnp.stack([cotangent] * lax.axis_size('fsdp')), 'fsdp', 0, 0)]
  transfers between devices with their start and end apart: 4 -> 4, of which waited for: 3 -> 2; matrix products, arithmetic and copies ran while one was open for 5% -> 7% of each run, Pallas kernels for 0% -> 0%
where the time goes in v1:
time: 806 us
  waiting for transfers between devices  717 us (89%)
  matrix products  50.7 us (6%)
  between operations  15.5 us (2%)
  starting transfers between devices  13 us (2%)
    all_gather x1, waiting for transfers between devices, local(): lax.all_gather(tokens_in, 'fsdp', axis=0, tiled=True)  368 us
    reduce_scatter x1, waiting for transfers between devices, local(): lax.psum_scatter((jnp.dot(gate_grad, w_gate, preferred_element_type=jnp.f...  347 us
  transfers between devices with their start and end apart: 4, of which 2 were waited for; matrix products, arithmetic and copies ran while one was open for 7% of the time, Pallas kernels for 0%

profile of v1, /device:TPU:16, one launch (start us, length us, event | category | flops | bytes accessed | tf_op | source)
XLA Modules:
  0.0 805.7 jit_solution(3723438214144191304)
XLA Ops:
  8.0 0.0 copy-start
  8.0 0.0 all-gather.2.cloned.1.call-start
  8.1 0.7 all-gather.2.cloned.1.call-update
  8.7 5.2 stack.2
  13.9 12.9 %all-to-all-start = ((bf16[64,16,4096]{2,1,0:T(8,128)(2,1)}), bf16[64,16,4096]{2,1,0:T(8,128)(2,1)}, u32[]{:S(2)}, u32[]{:S(2)}) async-start(bf16[64,16,4096]{2,1,0:T(8,128)(2,1)} %stack.2), calls=%async_computation | async-start | bytes 16777216 | tf_op jit(solution)/shard_map/all_to_all | solution.py:47
  26.9 0.0 all-reduce.2.cloned.1.call-start
  26.9 0.5 all-reduce.2.cloned.1.call-update
  27.4 0.0 reduce-scatter.2.cloned.1.call-start
  27.5 368.2 %all-gather.2.cloned.1.call-done = bf16[1024,4096]{1,0:T(8,128)(2,1)} async-done(((bf16[16,4096]{1,0:T(8,128)(2,1)}), bf16[1024,4096]{1,0:T(8,128)(2,1)}) %all-gather.2.cloned.1.call-update) | async-done | bytes 8388624 | tf_op jit(solution)/shard_map/all_gather | solution.py:45
  395.7 0.0 copy-done
  395.7 6.2 convolution_multiply_fusion
  401.9 0.0 all-to-all-done
  401.9 0.0 copy-start.2
  402.0 7.3 multiply_convert_fusion
  409.3 0.0 copy-done.2
  409.3 14.6 %fusion.5 = f32[1024,4096]{1,0:T(8,128)} fusion(f32[1024,112]{0,1:T(8,128)} %get-tuple-element.12, bf16[1024,4096]{1,0:T(8,128)(2,1)} %all-gather.2.cloned.1.call-done, bf16[1,112,4096]{2,1,0:T(8,128)(2,1)S(1)} %copy-done, f32[1024,112]{0,1:T(8,128)S(1)} %convolution_multiply_fusion, f32[1,112,4096]{2,1,0:T(8,128)S(1)} %copy-done.2), kind=kOutput, calls=%fused_computation.12 | convolution fusion | flops 1880768512 | bytes 28835840 | tf_op jit(solution)/shard_map/dot_general | solution.py:64
  423.9 13.9 %add_multiply_fusion = f32[1024,4096]{1,0:T(8,128)} fusion(f32[1024,4096]{1,0:T(8,128)} %fusion.5, bf16[1024,112]{0,1:T(8,128)(2,1)S(1)} %get-tuple-element.11, f32[1,112,4096]{2,1,0:T(8,128)S(1)} %copy-done.2), kind=kOutput, calls=%fused_computation | convolution fusion | flops 948371456 | bytes 35618816 | tf_op jit(solution)/shard_map/dot_general | solution.py:65
  437.8 0.0 copy-start.3
  437.8 0.0 copy-start.4
  437.8 0.0 reduce-scatter.2.cloned.1.call-update
  437.8 0.0 all-reduce.2.cloned.1.call-done
  437.8 0.9 copy-done.3
  438.7 0.1 copy-done.4
  438.8 1.8 multiply_subtract_fusion
  440.6 0.0 copy-start.1
  440.6 8.7 %convert_bitcast_fusion = (bf16[1,112,4096]{2,1,0:T(8,128)(2,1)}, f32[1,112,4096]{2,1,0:T(8,128)}, bf16[1,112,4096]{2,1,0:T(8,128)(2,1)}) fusion(bf16[1,112,4096]{2,1,0:T(8,128)(2,1)} %param.16, bf16[1,112,4096]{2,1,0:T(8,128)(2,1)} %param.15, f32[1,112,4096]{2,1,0:T(8,128)S(1)} %copy-done.2, bf16[1024,112]{0,1:T(8,128)(2,1)S(1)} %get-tuple-element.11, ...), kind=kOutput, calls=%fused_computation.20 | convolution fusion | flops 947781632 | bytes 15958016 | tf_op jit(solution)/shard_map/dot_general | solution.py:57
  449.3 347.3 %reduce-scatter.2.cloned.1.call-done = f32[16,4096]{1,0:T(8,128)} async-done(((f32[1024,4096]{1,0:T(8,128)}), f32[16,4096]{1,0:T(8,128)}) %reduce-scatter.2.cloned.1.call-update) | async-done | bytes 262160 | tf_op jit(solution)/shard_map/reduce_scatter | solution.py:62
  796.6 1.6 convert_element_type.38
  798.2 0.0 copy-done.1
Async XLA Ops:
  8.0 387.7 %copy-start = (bf16[1,112,4096]{2,1,0:T(8,128)(2,1)S(1)}, bf16[1,112,4096]{2,1,0:T(8,128)(2,1)}, u32[]{:S(2)}) copy-start(bf16[1,112,4096]{2,1,0:T(8,128)(2,1)} %param.12) | copy-start | bytes 2752516
  8.0 387.7 %all-gather.2.cloned.1.call-start = ((), (), s32[]{:S(2)}) async-start(), calls=%async_computation.2 | async-start | bytes 8519680 | tf_op jit(solution)/shard_map/all_gather | solution.py:45
  13.9 388.0 %all-to-all-start = ((bf16[64,16,4096]{2,1,0:T(8,128)(2,1)}), bf16[64,16,4096]{2,1,0:T(8,128)(2,1)}, u32[]{:S(2)}, u32[]{:S(2)}) async-start(bf16[64,16,4096]{2,1,0:T(8,128)(2,1)} %stack.2), calls=%async_computation | async-start | bytes 16777216 | tf_op jit(solution)/shard_map/all_to_all | solution.py:47
  26.9 411.0 %all-reduce.2.cloned.1.call-start = ((), (), s32[]{:S(2)}) async-start(), calls=%async_computation.4 | async-start | bytes 1048576 | tf_op jit(solution)/shard_map/psum | solution.py:80
  27.4 769.2 %reduce-scatter.2.cloned.1.call-start = ((), (), s32[]{:S(2)}) async-start(), calls=%async_computation.3 | async-start | bytes 17039360 | tf_op jit(solution)/shard_map/reduce_scatter | solution.py:62
  401.9 7.3 copy-start.2
  437.8 0.9 copy-start.3
  437.8 1.0 copy-start.4
  440.6 357.7 %copy-start.1 = (bf16[1,112,4096]{2,1,0:T(8,128)(2,1)S(1)}, bf16[1,112,4096]{2,1,0:T(8,128)(2,1)}, u32[]{:S(2)}) copy-start(bf16[1,112,4096]{2,1,0:T(8,128)(2,1)} %param.12) | copy-start | bytes 2752516
Sparse Core Ops, SparseCore 0:
  10.6 385.0 all-gather.1
  437.9 358.6 reduce-scatter.1
Sparse Core Ops, SparseCore 1:
  30.0 95.0 all-reduce.1
